TPU v7x, 32 devices: a whole 2x2x4 slice. The times are simulated.
32 devices in a mesh: dp: 8 (over z, x), tensor: 4 (over y, core).
Axes of the slice: x: 2, y: 2, z: 4, core: 2. Of those that a mesh axis runs over, the one named last changes fastest.
Arguments:
- tokens_in: bfloat16 [12288, 768], P('dp'), may hold values from -6 to 6
- cotangent: bfloat16 [12288, 768], P('dp'), may hold values from -6 to 6
- span_mask: int32 [12288], P('dp'), may hold values from 0 to 1, as said below
- lengths: int32 [24], P('dp'), may hold values from 128 to 512, as said below
- step: int32 [1], replicated, may hold values from 1000 to 31999
- warmup: int32 [1], replicated, may hold values from 1000 to 29999
- total: int32 [1], replicated, may hold values from 32000 to 40000
- w_qkv: float32 [768, 3, 768], P(None, None, 'tensor'), may hold values from -0.21875 to 0.21875
- w_out: float32 [768, 768], P(None, 'tensor'), may hold values from -1.25 to 1.25
- w_in: float32 [768, 3072], P(None, 'tensor'), may hold values from -0.21875 to 0.21875
- w_back: float32 [768, 3072], P(None, 'tensor'), may hold values from -0.109375 to 0.109375
- gains: float32 [2, 768], replicated, may hold values from 0.5 to 1.5
- biases: float32 [6, 768], replicated, may hold values from -3 to 3
- bias_in: float32 [3072], replicated, may hold values from -3 to 3
- mom_qkv: float32 [2, 768, 3, 768], P(None, 'dp', None, 'tensor'), as said below
- mom_out: float32 [2, 768, 768], P(None, 'dp', 'tensor'), as said below
- mom_in: float32 [2, 768, 3072], P(None, 'dp', 'tensor'), as said below
- mom_back: float32 [2, 768, 3072], P(None, 'dp', 'tensor'), as said below
- mom_gains: float32 [2, 2, 768], replicated, as said below
- mom_biases: float32 [2, 6, 768], replicated, as said below
- mom_bias_in: float32 [2, 3072], replicated, as said below
Outputs:
- normed_out: bfloat16 [12288, 768], P('dp')
- input_grad: float32 [12288, 768], P('dp')
- change_qkv: float32 [768, 3, 768], P(None, None, 'tensor')
- change_out_proj: float32 [768, 768], P(None, 'tensor')
- change_in_proj: float32 [768, 3072], P(None, 'tensor')
- change_back_proj: float32 [768, 3072], P(None, 'tensor')
- change_gains: float32 [2, 768], replicated
- change_biases: float32 [6, 768], replicated
- change_bias_in: float32 [3072], replicated
- new_mom_qkv: float32 [2, 768, 3, 768], P(None, 'dp', None, 'tensor')
- new_mom_out: float32 [2, 768, 768], P(None, 'dp', 'tensor')
- new_mom_in: float32 [2, 768, 3072], P(None, 'dp', 'tensor')
- new_mom_back: float32 [2, 768, 3072], P(None, 'dp', 'tensor')
- new_mom_gains: float32 [2, 2, 768], replicated
- new_mom_biases: float32 [2, 6, 768], replicated
- new_mom_bias_in: float32 [2, 3072], replicated
Inputs may be any that keep to these rules, and one draw needn't show every extreme that they name: `span_mask`: marked positions lie below their sequence's length and form unions of spans of 1 to 10 positions; each sequence has at most 76 of them, and in every draw each of the 3 sequences of some index of dp has exactly 76. `lengths`: a sequence's real tokens stand at its start, the rest is padding. step < total. warmup < total. `mom_qkv`: index 1 of the leading dimension holds positive second moments. `mom_out`: index 1 of the leading dimension holds positive second moments. `mom_in`: index 1 of the leading dimension holds positive second moments. `mom_back`: index 1 of the leading dimension holds positive second moments. `mom_gains`: index 1 of the leading dimension holds positive second moments. `mom_biases`: index 1 of the leading dimension holds positive second moments. `mom_bias_in`: index 1 of the leading dimension holds positive second moments.
All inputs are finite; a program needn't handle non-finite values.
Results may differ from a plain program's by a relative error of at most 0.017.
The roundings to bfloat16 on the way count: a program that leaves them out, or rounds other values in their place, can miss the bound.
Values sent between devices are 32-bit elements; how exact they have to be, the bound alone decides.
A program may use at most 128 MiB of HBM per device.

v0:
```python
import math
import jax
import jax.numpy as jnp
from jax import lax
from jax.sharding import PartitionSpec as P

HD = 64
SPAN_ROWS = 80
NORM_EPS = 1e-12
BETA_ONE = 0.9
BETA_TWO = 0.999
ADAM_EPS = 1e-06
WEIGHT_DECAY = 0.01


def layer_norm(values, gain, shift):
    center = values - jnp.mean(values, axis=-1, keepdims=True)
    spread = jnp.mean(center * center, axis=-1, keepdims=True)
    return center * lax.rsqrt(spread + NORM_EPS) * gain + shift


def exact_gelu(values):
    return jax.nn.gelu(values, approximate=False)


def outer_sum(left, right):
    return jnp.einsum("ta,tb->ab", left, right, preferred_element_type=jnp.float32)


def adam_step(weight, grad, moments, ratio, corr_one, corr_two, decay):
    first = BETA_ONE * moments[0] + (1.0 - BETA_ONE) * grad
    second = BETA_TWO * moments[1] + (1.0 - BETA_TWO) * grad * grad
    update = first / corr_one / (jnp.sqrt(second / corr_two) + ADAM_EPS) + decay * weight
    return (-ratio * update, jnp.stack([first, second]))


def on_device(
    tokens_in,
    cotangent,
    span_mask,
    lengths,
    step,
    warmup,
    total,
    w_qkv,
    w_out,
    w_in,
    w_back,
    gains,
    biases,
    bias_in,
    mom_qkv,
    mom_out,
    mom_in,
    mom_back,
    mom_gains,
    mom_biases,
    mom_bias_in,
):
    row_count, model_width = tokens_in.shape
    seq_count = lengths.shape[0]
    seq_length = row_count // seq_count
    head_cols = w_qkv.shape[2]
    hidden_cols = w_in.shape[1]
    head_size = HD
    local_heads = head_cols // head_size
    query_scale = 1.0 / math.sqrt(head_size)
    tensor_slot = lax.axis_index("tensor")
    bias_query = lax.dynamic_slice_in_dim(biases[0], tensor_slot * head_cols, head_cols)
    bias_value = lax.dynamic_slice_in_dim(biases[1], tensor_slot * head_cols, head_cols)
    bias_hidden = lax.dynamic_slice_in_dim(bias_in, tensor_slot * hidden_cols, hidden_cols)
    qkv_low = w_qkv.astype(jnp.bfloat16).reshape(model_width, 3 * head_cols)
    out_low = w_out.astype(jnp.bfloat16)
    in_low = w_in.astype(jnp.bfloat16)
    down_low = w_back.astype(jnp.bfloat16)
    projected = jnp.dot(tokens_in, qkv_low, preferred_element_type=jnp.float32).reshape(
        row_count, 3, head_cols
    )
    attn_shape = (seq_count, seq_length, local_heads, head_size)
    queries = (
        ((projected[:, 0] + bias_query) * query_scale).astype(jnp.bfloat16).reshape(attn_shape)
    )
    keys = projected[:, 1].astype(jnp.bfloat16).reshape(attn_shape)
    values = (projected[:, 2] + bias_value).astype(jnp.bfloat16).reshape(attn_shape)
    positions = jnp.arange(seq_length, dtype=jnp.int32)
    inside = positions[None, :] < lengths[:, None]
    key_bias = jnp.where(inside, 0.0, -1000000000.0).astype(jnp.float32)

    def score_block():
        raw = jnp.einsum("sqhd,skhd->shqk", queries, keys, preferred_element_type=jnp.float32)
        return raw + key_bias[:, None, None, :]

    scores = score_block()
    peak = jnp.max(scores, axis=-1, keepdims=True)
    log_total = peak + jnp.log(jnp.sum(jnp.exp(scores - peak), axis=-1, keepdims=True))
    probs_low = jnp.exp(scores - log_total).astype(jnp.bfloat16)
    context_low = (
        jnp.einsum("shqk,skhd->sqhd", probs_low, values, preferred_element_type=jnp.float32)
        .reshape(row_count, head_cols)
        .astype(jnp.bfloat16)
    )
    attn_part = jnp.einsum("tc,dc->td", context_low, out_low, preferred_element_type=jnp.float32)
    attn_sum = lax.psum(attn_part, "tensor")
    residual_one = tokens_in.astype(jnp.float32) + attn_sum + biases[2]
    normed = layer_norm(residual_one, gains[0], biases[3])
    normed_low = normed.astype(jnp.bfloat16)
    pre_act = jnp.dot(normed_low, in_low, preferred_element_type=jnp.float32) + bias_hidden
    act_low = exact_gelu(pre_act).astype(jnp.bfloat16)
    down_part = jnp.einsum("tf,df->td", act_low, down_low, preferred_element_type=jnp.float32)
    down_sum = lax.psum(down_part, "tensor")
    residual_two = normed + down_sum + biases[4]
    live = inside.astype(jnp.int32) * span_mask.reshape(seq_count, seq_length) > 0
    upto = (positions[:, None] <= positions[None, :]).astype(jnp.float32)
    rank = jnp.dot(live.astype(jnp.float32), upto).astype(jnp.int32) - 1
    slots = jnp.arange(SPAN_ROWS, dtype=jnp.int32)
    pick = (live[:, None, :] & (rank[:, None, :] == slots[None, :, None])).astype(jnp.float32)
    pick_low = pick.astype(jnp.bfloat16)

    def rows_of(values):
        width = values.shape[-1]
        return jnp.einsum(
            "srt,std->srd",
            pick,
            values.reshape(seq_count, seq_length, width),
            precision=lax.Precision.HIGHEST,
        ).reshape(seq_count * SPAN_ROWS, width)

    def low_rows_of(values):
        width = values.shape[-1]
        return jnp.einsum(
            "srt,std->srd",
            pick_low,
            values.reshape(seq_count, seq_length, width),
            preferred_element_type=jnp.bfloat16,
        ).reshape(seq_count * SPAN_ROWS, width)

    result = layer_norm(residual_two, gains[1], biases[5])
    normed_out = result.astype(jnp.bfloat16)
    residual_one_rows = rows_of(residual_one)
    residual_two_rows = rows_of(residual_two)
    grad_result = low_rows_of(cotangent).astype(jnp.float32)
    _, norm_two_back = jax.vjp(layer_norm, residual_two_rows, gains[1], biases[5])
    d_res_two, d_gain_two, d_shift_two = norm_two_back(grad_result)
    d_res_two_low = d_res_two.astype(jnp.bfloat16)
    normed_low_rows = low_rows_of(normed_low)
    pre_rows = jnp.dot(normed_low_rows, in_low, preferred_element_type=jnp.float32) + bias_hidden
    act_rows, gelu_back = jax.vjp(exact_gelu, pre_rows)
    grad_back = outer_sum(d_res_two_low, act_rows.astype(jnp.bfloat16))
    d_act = jnp.dot(d_res_two_low, down_low, preferred_element_type=jnp.float32)
    d_pre = gelu_back(d_act)[0]
    d_pre_low = d_pre.astype(jnp.bfloat16)
    grad_in = outer_sum(normed_low_rows, d_pre_low)
    d_normed_part = jnp.einsum("tf,df->td", d_pre_low, in_low, preferred_element_type=jnp.float32)
    d_normed = lax.psum(d_normed_part, "tensor") + d_res_two
    _, norm_one_back = jax.vjp(layer_norm, residual_one_rows, gains[0], biases[3])
    d_res_one, d_gain_one, d_shift_one = norm_one_back(d_normed)
    d_res_one_low = d_res_one.astype(jnp.bfloat16)
    grad_out_proj = outer_sum(d_res_one_low, low_rows_of(context_low))
    row_shape = (seq_count, SPAN_ROWS, local_heads, head_size)
    d_context = (
        jnp.dot(d_res_one_low, out_low, preferred_element_type=jnp.float32)
        .astype(jnp.bfloat16)
        .reshape(row_shape)
    )
    query_rows = low_rows_of(queries.reshape(row_count, head_cols)).reshape(row_shape)
    raw = jnp.einsum("sqhd,skhd->shqk", query_rows, keys, preferred_element_type=jnp.float32)
    probs = jax.nn.softmax(raw + key_bias[:, None, None, :], axis=-1)
    probs_again = probs.astype(jnp.bfloat16)
    d_probs = jnp.einsum("sqhd,skhd->shqk", d_context, values, preferred_element_type=jnp.float32)
    d_values = jnp.einsum(
        "shqk,sqhd->skhd", probs_again, d_context, preferred_element_type=jnp.float32
    ).reshape(row_count, head_cols)
    d_scores = (probs * (d_probs - jnp.sum(probs * d_probs, axis=-1, keepdims=True))).astype(
        jnp.bfloat16
    )
    d_queries = (
        jnp.einsum("shqk,skhd->sqhd", d_scores, keys, preferred_element_type=jnp.float32).reshape(
            seq_count * SPAN_ROWS, head_cols
        )
        * query_scale
    )
    d_keys = jnp.einsum(
        "shqk,sqhd->skhd", d_scores, query_rows, preferred_element_type=jnp.float32
    ).reshape(row_count, head_cols)

    def spread(row_values):
        width = row_values.shape[-1]
        return jnp.einsum(
            "srt,srd->std",
            pick,
            row_values.reshape(seq_count, SPAN_ROWS, width),
            precision=lax.Precision.HIGHEST,
        ).reshape(row_count, width)

    d_proj_low = (
        jnp.stack([spread(d_queries), d_keys, d_values], axis=1)
        .astype(jnp.bfloat16)
        .reshape(row_count, 3 * head_cols)
    )
    grad_qkv = outer_sum(tokens_in, d_proj_low).reshape(model_width, 3, head_cols)
    d_entry_part = jnp.einsum("tc,dc->td", d_proj_low, qkv_low, preferred_element_type=jnp.float32)
    input_grad = lax.psum(d_entry_part, "tensor") + spread(d_res_one)
    first_rank = (tensor_slot == 0).astype(jnp.float32)
    width_zero = jnp.zeros((model_width,), jnp.float32)

    def place_heads(partial_sum):
        return lax.dynamic_update_slice_in_dim(width_zero, partial_sum, tensor_slot * head_cols, 0)

    grad_gains = jnp.stack([d_gain_one, d_gain_two]) * first_rank
    grad_biases = jnp.stack(
        [
            place_heads(jnp.sum(d_queries, axis=0)),
            place_heads(jnp.sum(d_values, axis=0)),
            jnp.sum(d_res_one, axis=0) * first_rank,
            d_shift_one * first_rank,
            jnp.sum(d_res_two, axis=0) * first_rank,
            d_shift_two * first_rank,
        ]
    )
    grad_bias_in = lax.dynamic_update_slice_in_dim(
        jnp.zeros(bias_in.shape, jnp.float32), jnp.sum(d_pre, axis=0), tensor_slot * hidden_cols, 0
    )
    grad_gains, grad_biases, grad_bias_in = lax.psum(
        (grad_gains, grad_biases, grad_bias_in), ("dp", "tensor")
    )
    data_slot = lax.axis_index("dp")
    shard_rows = model_width // lax.axis_size("dp")
    owned = tuple(
        (
            lax.psum_scatter(part, "dp", scatter_dimension=0, tiled=True)
            for part in (grad_qkv, grad_out_proj, grad_in, grad_back)
        )
    )
    clock = step[0].astype(jnp.float32)
    warm = warmup[0].astype(jnp.float32)
    horizon = total[0].astype(jnp.float32)
    ratio = jnp.minimum(clock / warm, (horizon - clock) / (horizon - warm))
    corr_one = 1.0 - jnp.power(BETA_ONE, clock)
    corr_two = 1.0 - jnp.power(BETA_TWO, clock)
    change_rows = []
    fresh_moments = []
    for weight, grad_rows, moment in zip(
        (w_qkv, w_out, w_in, w_back), owned, (mom_qkv, mom_out, mom_in, mom_back)
    ):
        weight_rows = lax.dynamic_slice_in_dim(weight, data_slot * shard_rows, shard_rows, 0)
        row_change, new_moment = adam_step(
            weight_rows, grad_rows, moment, ratio, corr_one, corr_two, WEIGHT_DECAY
        )
        change_rows.append(row_change)
        fresh_moments.append(new_moment)
    change_qkv, change_out_proj, change_in_proj, change_back_proj = (
        lax.all_gather(change_rows[0], "dp", axis=0, tiled=True),
        lax.all_gather(change_rows[1], "dp", axis=0, tiled=True),
        lax.all_gather(change_rows[2], "dp", axis=0, tiled=True),
        lax.all_gather(change_rows[3], "dp", axis=0, tiled=True),
    )
    change_gains, new_mom_gains = adam_step(
        gains, grad_gains, mom_gains, ratio, corr_one, corr_two, 0.0
    )
    change_biases, new_mom_biases = adam_step(
        biases, grad_biases, mom_biases, ratio, corr_one, corr_two, 0.0
    )
    change_bias_in, new_mom_bias_in = adam_step(
        bias_in, grad_bias_in, mom_bias_in, ratio, corr_one, corr_two, 0.0
    )
    return (
        normed_out,
        input_grad,
        change_qkv,
        change_out_proj,
        change_in_proj,
        change_back_proj,
        change_gains,
        change_biases,
        change_bias_in,
        fresh_moments[0],
        fresh_moments[1],
        fresh_moments[2],
        fresh_moments[3],
        new_mom_gains,
        new_mom_biases,
        new_mom_bias_in,
    )


def solution(mesh):
    in_specs = (
        P("dp", None),
        P("dp", None),
        P("dp"),
        P("dp"),
        P(),
        P(),
        P(),
        P(None, None, "tensor"),
        P(None, "tensor"),
        P(None, "tensor"),
        P(None, "tensor"),
        P(),
        P(),
        P(),
        P(None, "dp", None, "tensor"),
        P(None, "dp", "tensor"),
        P(None, "dp", "tensor"),
        P(None, "dp", "tensor"),
        P(),
        P(),
        P(),
    )
    out_specs = (
        P("dp", None),
        P("dp", None),
        P(None, None, "tensor"),
        P(None, "tensor"),
        P(None, "tensor"),
        P(None, "tensor"),
        P(),
        P(),
        P(),
        P(None, "dp", None, "tensor"),
        P(None, "dp", "tensor"),
        P(None, "dp", "tensor"),
        P(None, "dp", "tensor"),
        P(),
        P(),
        P(),
    )
    return jax.shard_map(
        on_device, mesh=mesh, in_specs=in_specs, out_specs=out_specs, check_vma=False
    )
```

profile of v0, /device:TPU:0, one launch (start us, length us, event | category | flops | bytes accessed | tf_op | source)
XLA Modules:
  0.0 894.0 jit_solution(5073173420024962855)
XLA Ops:
  7.2 3.9 fusion.15
  13.9 2.1 convert_element_type.129
  18.3 1.8 fusion.168
  22.7 2.8 add_reduce_fusion
  27.3 1.8 copy-done.3
  29.8 2.8 squeeze.6
  34.5 5.7 fusion.20
  41.2 3.0 fusion.96
  46.6 94.5 %all-reduce.6.cloned.1.call-done = f32[1536,768]{1,0:T(8,128)} async-done(((f32[1536,768]{1,0:T(8,128)}), f32[1536,768]{1,0:T(8,128)}) %all-reduce.6.cloned.1.call-update) | async-done | bytes 4718608 | tf_op jit(solution)/shard_map/psum | solution.py:103
  141.1 3.8 fusion.167
  147.1 2.1 fusion.14
  149.2 17.8 %fusion.18 = f32[1536,768]{1,0:T(8,128)} fusion(bf16[1536,768]{1,0:T(8,128)(2,1)} %fusion.14, f32[768]{0:T(1024)} %dynamic_slice.23, f32[768,768]{1,0:T(8,128)} %param.31, f32[768,768]{1,0:T(8,128)} %param.30), kind=kOutput, calls=%fused_computation.39 | convolution fusion | flops 3702915072 | bytes 11799552 | tf_op jit(solution)/shard_map/tf,df->td/dot_general | solution.py:109
  170.6 2.0 fusion.35
  172.6 3.1 fusion.175
  175.7 4.6 fusion.173
  183.3 78.0 %all-reduce.8.cloned.1.call-done = f32[1536,768]{1,0:T(8,128)} async-done(((f32[1536,768]{1,0:T(8,128)}), f32[1536,768]{1,0:T(8,128)}) %all-reduce.8.cloned.1.call-update) | async-done | bytes 4718608 | tf_op jit(solution)/shard_map/psum | solution.py:110
  261.3 5.3 fusion.166
  266.7 2.2 copy-done.4
  268.9 2.1 fusion.174
  271.0 2.0 multiply_reduce_fusion.8
  276.3 4.8 fusion.180
  283.3 33.8 %all-reduce.10.cloned.1.call-done = f32[240,768]{1,0:T(8,128)} async-done(((f32[240,768]{1,0:T(8,128)}), f32[240,768]{1,0:T(8,128)}) %all-reduce.10.cloned.1.call-update) | async-done | bytes 737296 | tf_op jit(solution)/shard_map/psum | solution.py:154
  317.0 2.2 fusion.163
  323.2 2.6 fusion.179
  339.3 4.4 fusion.181
  343.7 3.0 copy.97
  346.8 1.9 fusion.89
  348.8 4.6 fusion.62
  355.3 6.1 convolution_bitcast_fusion
  365.0 51.3 %reduce-scatter.5.cloned.1.call-done = f32[96,3,192]{2,0,1:T(8,128)} async-done(((f32[768,3,192]{2,0,1:T(8,128)}), f32[96,3,192]{2,0,1:T(8,128)}) %reduce-scatter.5.cloned.1.call-update) | async-done | bytes 221200 | tf_op jit(solution)/shard_map/reduce_scatter | solution.py:230
  416.3 2.2 fusion.104
  418.5 69.8 %reduce-scatter.9.cloned.1.call-done = f32[96,768]{1,0:T(8,128)} async-done(((f32[768,768]{1,0:T(8,128)}), f32[96,768]{1,0:T(8,128)}) %reduce-scatter.9.cloned.1.call-update) | async-done | bytes 294928 | tf_op jit(solution)/shard_map/reduce_scatter | solution.py:230
  488.3 2.2 fusion.105
  492.8 3.0 multiply_reduce_fusion
  495.9 4.2 add_convert_fusion
  500.1 59.7 %reduce-scatter.11.cloned.1.call-done = f32[96,768]{1,0:T(8,128)} async-done(((f32[768,768]{1,0:T(8,128)}), f32[96,768]{1,0:T(8,128)}) %reduce-scatter.11.cloned.1.call-update) | async-done | bytes 294928 | tf_op jit(solution)/shard_map/reduce_scatter | solution.py:230
  559.9 2.0 fusion.106
  562.9 40.3 %all-reduce = (f32[2,768]{1,0:T(2,128)S(1)}, f32[6,768]{1,0:T(8,128)S(1)}, f32[3072]{0:T(1024)S(1)}) all-reduce(f32[2,768]{1,0:T(2,128)S(1)} %maximum_multiply_fusion, f32[6,768]{1,0:T(8,128)S(1)} %stack.88, f32[3072]{0:T(1024)S(1)} %dynamic_update_slice.13), channel_id=1, replica_groups=mesh['dp'=8,'tensor'=4] {'dp','tensor'}, use_global_device_ids=true, to_apply=%region_27.28 | all-reduce | flops 9216 | bytes 73728 | tf_op jit(solution)/shard_map/psum | solution.py:223
  607.0 4.3 fusion.47
  611.3 13.9 %reduce-scatter.7.cloned.1.call-done = f32[96,192]{1,0:T(8,128)} async-done(((f32[768,192]{1,0:T(8,128)}), f32[96,192]{1,0:T(8,128)}) %reduce-scatter.7.cloned.1.call-update) | async-done | bytes 73744 | tf_op jit(solution)/shard_map/reduce_scatter | solution.py:230
  626.3 32.2 %all_gather.13 = f32[768,192]{1,0:T(8,128)S(1)} all-gather(f32[96,192]{1,0:T(8,128)S(1)} %get-tuple-element.107), channel_id=1, replica_groups=mesh['dp'=8,'tensor'=4] {'dp'}, dimensions={0}, use_global_device_ids=true | all-gather | bytes 663552 | tf_op jit(solution)/shard_map/all_gather | solution.py:253
  660.3 60.5 %all-reduce.12.cloned.1.call-done = f32[1536,768]{1,0:T(8,128)} async-done(((f32[1536,768]{1,0:T(8,128)}), f32[1536,768]{1,0:T(8,128)}) %all-reduce.12.cloned.1.call-update) | async-done | bytes 4718608 | tf_op jit(solution)/shard_map/psum | solution.py:202
  720.8 6.6 bitcast_add_fusion
  729.9 46.0 %all-gather.4.cloned.1.call-done = f32[768,3,192]{2,0,1:T(8,128)} async-done(((f32[96,3,192]{2,0,1:T(8,128)}), f32[768,3,192]{2,0,1:T(8,128)}) %all-gather.4.cloned.1.call-update) | async-done | bytes 1769488 | tf_op jit(solution)/shard_map/all_gather | solution.py:252
  775.9 2.9 copy.102
  778.8 50.6 %all-gather.6.cloned.1.call-done = f32[768,768]{1,0:T(8,128)} async-done(((f32[96,768]{1,0:T(8,128)}), f32[768,768]{1,0:T(8,128)}) %all-gather.6.cloned.1.call-update) | async-done | bytes 2359312 | tf_op jit(solution)/shard_map/all_gather | solution.py:254
  829.4 53.1 %all-gather.8.cloned.1.call-done = f32[768,768]{1,0:T(8,128)} async-done(((f32[96,768]{1,0:T(8,128)}), f32[768,768]{1,0:T(8,128)}) %all-gather.8.cloned.1.call-update) | async-done | bytes 2359312 | tf_op jit(solution)/shard_map/all_gather | solution.py:255
  882.5 3.4 copy.181
  (253 shorter events, 64.1 us)
Async XLA Ops:
  7.2 263.8 %copy-start = (bf16[1536,768]{1,0:T(8,128)(2,1)S(1)}, bf16[1536,768]{1,0:T(8,128)(2,1)}, u32[]{:S(2)}) copy-start(bf16[1536,768]{1,0:T(8,128)(2,1)} %param.22) | copy-start | bytes 7077892
  7.2 133.9 %all-reduce.6.cloned.1.call-start = ((), (), s32[]{:S(2)}) async-start(), calls=%async_computation.4 | async-start | bytes 9437184 | tf_op jit(solution)/shard_map/psum | solution.py:103
  25.5 7.0 copy-start.60
  34.4 6.7 copy-start.19
  44.2 217.1 %all-reduce.8.cloned.1.call-start = ((), (), s32[]{:S(2)}) async-start(), calls=%async_computation.5 | async-start | bytes 9437184 | tf_op jit(solution)/shard_map/psum | solution.py:110
  167.0 150.0 %all-reduce.10.cloned.1.call-start = ((), (), s32[]{:S(2)}) async-start(), calls=%async_computation.6 | async-start | bytes 1474560 | tf_op jit(solution)/shard_map/psum | solution.py:154
  172.6 9.3 %copy-start.26 = (bf16[3,80,192]{1,2,0:T(8,128)(2,1)}, bf16[3,80,192]{1,2,0:T(8,128)(2,1)S(1)}, u32[]{:S(2)}) copy-start(bf16[3,80,192]{1,2,0:T(8,128)(2,1)S(1)} %fusion.35) | copy-start | bytes 276484
  175.7 6.2 copy-start.8
  175.7 6.2 copy-start.55
  180.3 81.0 %copy-start.31 = (f32[1536]{0:T(1024)S(1)}, f32[1536]{0:T(1024)}, u32[]{:S(2)}) copy-start(f32[1536]{0:T(1024)} %copy-done.30) | copy-start | bytes 18436
  180.3 81.0 %copy-start.35 = (f32[1536]{0:T(1024)S(1)}, f32[1536]{0:T(1024)}, u32[]{:S(2)}) copy-start(f32[1536]{0:T(1024)} %copy-done.34) | copy-start | bytes 18436
  180.3 81.0 %copy-start.40 = (f32[768]{0:T(1024)S(1)}, f32[768]{0:T(1024)}, u32[]{:S(2)}) copy-start(f32[768]{0:T(1024)} %get-tuple-element.118) | copy-start | bytes 9220
  180.3 81.0 %copy-start.57 = (f32[768]{0:T(1024)S(1)}, f32[768]{0:T(1024)}, u32[]{:S(2)}) copy-start(f32[768]{0:T(1024)} %get-tuple-element.119) | copy-start | bytes 9220
  273.2 7.9 copy-start.45
  273.2 7.9 copy-start.47
  274.6 6.4 copy-start.49
  282.5 133.8 %reduce-scatter.5.cloned.1.call-start = ((), (), s32[]{:S(2)}) async-start(), calls=%async_computation.8 | async-start | bytes 2654208 | tf_op jit(solution)/shard_map/reduce_scatter | solution.py:230
  330.9 8.4 copy-start.21
  346.7 141.6 %reduce-scatter.9.cloned.1.call-start = ((), (), s32[]{:S(2)}) async-start(), calls=%async_computation.11 | async-start | bytes 2654208 | tf_op jit(solution)/shard_map/reduce_scatter | solution.py:230
  348.8 211.1 %reduce-scatter.11.cloned.1.call-start = ((), (), s32[]{:S(2)}) async-start(), calls=%async_computation.13 | async-start | bytes 2654208 | tf_op jit(solution)/shard_map/reduce_scatter | solution.py:230
  353.4 271.8 %reduce-scatter.7.cloned.1.call-start = ((), (), s32[]{:S(2)}) async-start(), calls=%async_computation.10 | async-start | bytes 884736 | tf_op jit(solution)/shard_map/reduce_scatter | solution.py:230
  355.0 365.8 %all-reduce.12.cloned.1.call-start = ((), (), s32[]{:S(2)}) async-start(), calls=%async_computation.7 | async-start | bytes 9437184 | tf_op jit(solution)/shard_map/psum | solution.py:202
  361.3 130.4 %copy-start.38 = (f32[2,6,768]{2,0,1:T(2,128)S(1)}, f32[2,6,768]{2,0,1:T(2,128)}, u32[]{:S(2)}) copy-start(f32[2,6,768]{2,0,1:T(2,128)} %param.40) | copy-start | bytes 110596
  361.3 130.4 %copy-start.42 = (f32[2,3072]{1,0:T(2,128)S(1)}, f32[2,3072]{1,0:T(2,128)}, u32[]{:S(2)}) copy-start(f32[2,3072]{1,0:T(2,128)} %param.41) | copy-start | bytes 73732
  361.3 131.0 %copy-start.7 = (f32[3,80,768]{2,1,0:T(8,128)S(1)}, f32[3,80,768]{2,1,0:T(8,128)}, u32[]{:S(2)}) copy-start(f32[3,80,768]{2,1,0:T(8,128)} %get-tuple-element.137) | copy-start | bytes 2211844
  361.3 131.0 %copy-start.46 = (f32[3,80]{1,0:T(4,128)S(1)}, f32[3,80]{1,0:T(4,128)}, u32[]{:S(2)}) copy-start(f32[3,80]{1,0:T(4,128)} %copy-done.45) | copy-start | bytes 2884
  361.3 131.0 %copy-start.48 = (f32[3,80]{1,0:T(4,128)S(1)}, f32[3,80]{1,0:T(4,128)}, u32[]{:S(2)}) copy-start(f32[3,80]{1,0:T(4,128)} %copy-done.47) | copy-start | bytes 2884
  361.3 131.0 %copy-start.50 = (f32[3,80]{1,0:T(4,128)S(1)}, f32[3,80]{1,0:T(4,128)}, u32[]{:S(2)}) copy-start(f32[3,80]{1,0:T(4,128)} %copy-done.49) | copy-start | bytes 2884
  361.4 131.4 %copy-start.41 = (f32[1536]{0:T(1024)S(1)}, f32[1536]{0:T(1024)}, u32[]{:S(2)}) copy-start(f32[1536]{0:T(1024)} %get-tuple-element.88) | copy-start | bytes 18436
  361.4 414.5 %all-gather.4.cloned.1.call-start = ((), (), s32[]{:S(2)}) async-start(), calls=%async_computation.9 | async-start | bytes 2654208 | tf_op jit(solution)/shard_map/all_gather | solution.py:252
  418.4 77.3 %copy-start.51 = (f32[768]{0:T(1024)S(1)}, f32[768]{0:T(1024)}, u32[]{:S(2)}) copy-start(f32[768]{0:T(1024)} %get-tuple-element.120) | copy-start | bytes 9220
  418.5 410.9 %all-gather.6.cloned.1.call-start = ((), (), s32[]{:S(2)}) async-start(), calls=%async_computation.12 | async-start | bytes 2654208 | tf_op jit(solution)/shard_map/all_gather | solution.py:254
  490.5 392.0 %all-gather.8.cloned.1.call-start = ((), (), s32[]{:S(2)}) async-start(), calls=%async_computation.14 | async-start | bytes 2654208 | tf_op jit(solution)/shard_map/all_gather | solution.py:255
  495.7 64.1 %copy-start.28 = (f32[2,96,768]{2,1,0:T(8,128)S(1)}, f32[2,96,768]{2,1,0:T(8,128)}, u32[]{:S(2)}) copy-start(f32[2,96,768]{2,1,0:T(8,128)} %param.38) | copy-start | bytes 1769476
  495.8 66.1 %copy-start.56 = (f32[768]{0:T(1024)S(1)}, f32[768]{0:T(1024)}, u32[]{:S(2)}) copy-start(f32[768]{0:T(1024)} %get-tuple-element.70) | copy-start | bytes 9220
  495.8 66.2 %copy-start.59 = (f32[768]{0:T(1024)S(1)}, f32[768]{0:T(1024)}, u32[]{:S(2)}) copy-start(f32[768]{0:T(1024)} %get-tuple-element.146) | copy-start | bytes 9220
  495.8 66.5 %copy-start.52 = (f32[768]{0:T(1024)S(1)}, f32[768]{0:T(1024)}, u32[]{:S(2)}) copy-start(f32[768]{0:T(1024)} %get-tuple-element.66) | copy-start | bytes 9220
  495.8 66.5 %copy-start.62 = (f32[3,64]{1,0:T(4,128)S(1)}, f32[3,64]{1,0:T(4,128)}, u32[]{:S(2)}) copy-start(f32[3,64]{1,0:T(4,128)} %get-tuple-element.142) | copy-start | bytes 2308
  495.8 66.5 %copy-start.61 = (f32[3,64]{1,0:T(4,128)S(1)}, f32[3,64]{1,0:T(4,128)}, u32[]{:S(2)}) copy-start(f32[3,64]{1,0:T(4,128)} %get-tuple-element.144) | copy-start | bytes 2308
  495.8 66.6 %copy-start.54 = (f32[768]{0:T(1024)S(1)}, f32[768]{0:T(1024)}, u32[]{:S(2)}) copy-start(f32[768]{0:T(1024)} %get-tuple-element.85) | copy-start | bytes 9220
  495.8 66.6 %copy-start.53 = (f32[768]{0:T(1024)S(1)}, f32[768]{0:T(1024)}, u32[]{:S(2)}) copy-start(f32[768]{0:T(1024)} %get-tuple-element.71) | copy-start | bytes 9220
  495.9 107.4 %copy-start.33 = (f32[6,768]{1,0:T(8,128)S(1)}, f32[6,768]{1,0:T(8,128)}, u32[]{:S(2)}) copy-start(f32[6,768]{1,0:T(8,128)} %param.33) | copy-start | bytes 55300
  495.9 108.7 %copy-start.43 = (f32[2,768]{1,0:T(2,128)S(1)}, f32[2,768]{1,0:T(2,128)}, u32[]{:S(2)}) copy-start(f32[2,768]{1,0:T(2,128)} %param.32) | copy-start | bytes 18436
  495.9 108.7 %copy-start.58 = (f32[2,2,768]{2,1,0:T(2,128)S(1)}, f32[2,2,768]{2,1,0:T(2,128)}, u32[]{:S(2)}) copy-start(f32[2,2,768]{2,1,0:T(2,128)} %param.39) | copy-start | bytes 36868
  495.9 109.9 %copy-start.36 = (f32[1,3072]{1,0:T(1,128)S(1)}, f32[1,3072]{1,0:T(1,128)}, u32[]{:S(2)}) copy-start(f32[1,3072]{1,0:T(1,128)} %get-tuple-element.113) | copy-start | bytes 36868
  495.9 109.9 %copy-start.37 = (f32[1,3072]{1,0:T(1,128)S(1)}, f32[1,3072]{1,0:T(1,128)}, u32[]{:S(2)}) copy-start(f32[1,3072]{1,0:T(1,128)} %get-tuple-element.114) | copy-start | bytes 36868
  495.9 109.9 %copy-start.44 = (f32[3072]{0:T(1024)S(1)}, f32[3072]{0:T(1024)}, u32[]{:S(2)}) copy-start(f32[3072]{0:T(1024)} %param.34) | copy-start | bytes 36868
  660.3 67.1 %copy-start.25 = (f32[1,96,3,192]{3,1,2,0:T(8,128)S(1)}, f32[1,96,3,192]{3,1,2,0:T(8,128)}, u32[]{:S(2)}) copy-start(f32[1,96,3,192]{3,1,2,0:T(8,128)} %get-tuple-element.103) | copy-start | bytes 663556
  (27 other events, 78.4 us)
Sparse Core Ops, SparseCore 0:
  44.3 96.7 all-reduce.5
  167.1 94.1 all-reduce.7
  282.6 34.3 all-reduce.9
  346.9 69.3 reduce-scatter.4
  420.2 68.0 reduce-scatter.8
  491.6 68.1 reduce-scatter.10
  563.7 61.4 reduce-scatter.6
  627.8 92.9 all-reduce.11
  723.8 52.0 all-gather.3
  778.8 50.5 all-gather.5
  831.8 50.5 all-gather.7
where the time goes:
time: 903 us; the launch traced here: 894 us
  waiting for transfers between devices  611 us (68%)
  matrix products  86.9 us (10%)
  blocking collectives  72.5 us (8%)
  other arithmetic  56.1 us (6%)
  local copies, waits for them, and re-layouts  48.5 us (5%)
  between operations  17.2 us (2%)
    reduce_scatter x4, waiting for transfers between devices, on_device(): lax.psum_scatter(part, 'dp', scatter_dimension=0, tiled=True)  195 us
    psum x1, waiting for transfers between devices, on_device(): attn_sum = lax.psum(attn_part, 'tensor')  94.5 us
    psum x1, waiting for transfers between devices, on_device(): down_sum = lax.psum(down_part, 'tensor')  78 us
    psum x1, waiting for transfers between devices, on_device(): input_grad = lax.psum(d_entry_part, 'tensor') + spread(d_res_one)  60.5 us
    all_gather x1, waiting for transfers between devices, on_device(): lax.all_gather(change_rows[3], 'dp', axis=0, tiled=True)  53.1 us
    all_gather x1, waiting for transfers between devices, on_device(): lax.all_gather(change_rows[2], 'dp', axis=0, tiled=True)  50.6 us
    all_gather x1, waiting for transfers between devices, on_device(): lax.all_gather(change_rows[0], 'dp', axis=0, tiled=True)  46 us
    psum x1, blocking collectives, on_device(): lax.psum((grad_gains, grad_biases, grad_bias_in), ('dp', 'tensor'))  40.3 us
  transfers between devices with their start and end apart: 11, of which 11 were waited for; matrix products, arithmetic and copies ran while one was open for 8% of the time, Pallas kernels for 0%

commit v1 on v0

--- a/solution.py
+++ b/solution.py
@@ -11,6 +11,28 @@
 BETA_TWO = 0.999
 ADAM_EPS = 1e-06
 WEIGHT_DECAY = 0.01
+
+
+def joined_along(blocks, dim):
+    dims = list(blocks.shape[1:])
+    dims[dim] *= blocks.shape[0]
+    return jnp.moveaxis(blocks, 0, dim).reshape(dims)
+
+
+def doubled(x, axis):
+    length = lax.axis_size(axis)
+    blocks = x[None]
+    for level in range(length.bit_length() - 1):
+        apart = 1 << level
+        other = lax.ppermute(blocks, axis, [(i, i ^ apart) for i in range(length)])
+        both = jnp.stack([blocks, other])
+        upper = lax.axis_index(axis) >> level & 1
+        blocks = jnp.where(upper == 0, both, both[::-1]).reshape(-1, *x.shape)
+    return blocks
+
+
+def gather_by_bits(array, axis, dim):
+    return joined_along(doubled(array, axis), dim)
 
 
 def layer_norm(values, gain, shift):
@@ -252,7 +274,7 @@
         lax.all_gather(change_rows[0], "dp", axis=0, tiled=True),
         lax.all_gather(change_rows[1], "dp", axis=0, tiled=True),
         lax.all_gather(change_rows[2], "dp", axis=0, tiled=True),
-        lax.all_gather(change_rows[3], "dp", axis=0, tiled=True),
+        gather_by_bits(change_rows[3], "dp", 0),
     )
     change_gains, new_mom_gains = adam_step(
         gains, grad_gains, mom_gains, ratio, corr_one, corr_two, 0.0

time: 903 us -> 847 us (0.938)
  waiting for transfers between devices: 611 us -> 554 us
    all_gather x1 -> x0, waiting for transfers between devices: 53.1 us -> none  [on_device(): lax.all_gather(change_rows[3], 'dp', axis=0, tiled=True)]
  transfers between devices with their start and end apart: 11 -> 13, of which waited for: 11 -> 11; matrix products, arithmetic and copies ran while one was open for 8% -> 9% of each run, Pallas kernels for 0% -> 0%
where the time goes in v1:
time: 847 us; the launch traced here: 838 us
  waiting for transfers between devices  554 us (65%)
  matrix products  85.8 us (10%)
  blocking collectives  73.3 us (9%)
  other arithmetic  57 us (7%)
  local copies, waits for them, and re-layouts  47.5 us (6%)
  between operations  17.5 us (2%)
    reduce_scatter x4, waiting for transfers between devices, on_device(): lax.psum_scatter(part, 'dp', scatter_dimension=0, tiled=True)  188 us
    psum x1, waiting for transfers between devices, on_device(): attn_sum = lax.psum(attn_part, 'tensor')  94.5 us
    psum x1, waiting for transfers between devices, on_device(): down_sum = lax.psum(down_part, 'tensor')  78 us
    psum x1, waiting for transfers between devices, on_device(): input_grad = lax.psum(d_entry_part, 'tensor') + spread(d_res_one)  59 us
    all_gather x1, waiting for transfers between devices, on_device(): lax.all_gather(change_rows[2], 'dp', axis=0, tiled=True)  50.6 us
    all_gather x1, waiting for transfers between devices, on_device(): lax.all_gather(change_rows[0], 'dp', axis=0, tiled=True)  43.6 us
    psum x1, blocking collectives, on_device(): lax.psum((grad_gains, grad_biases, grad_bias_in), ('dp', 'tensor'))  40.9 us
    psum x1, waiting for transfers between devices, on_device(): d_normed = lax.psum(d_normed_part, 'tensor') + d_res_two  33.8 us
  transfers between devices with their start and end apart: 13, of which 11 were waited for; matrix products, arithmetic and copies ran while one was open for 9% of the time, Pallas kernels for 0%

profile of v1, /device:TPU:0, one launch (start us, length us, event | category | flops | bytes accessed | tf_op | source)
XLA Modules:
  0.0 837.9 jit_solution(15101758254510077992)
XLA Ops:
  7.2 3.9 fusion.15
  13.9 2.1 convert_element_type.129
  18.3 1.8 fusion.170
  20.9 1.8 multiply_convert_fusion
  22.7 2.8 add_reduce_fusion
  27.3 1.9 copy-done.3
  29.8 2.8 squeeze.6
  34.5 5.7 fusion.20
  41.2 3.0 fusion.98
  46.6 94.5 %all-reduce.6.cloned.1.call-done = f32[1536,768]{1,0:T(8,128)} async-done(((f32[1536,768]{1,0:T(8,128)}), f32[1536,768]{1,0:T(8,128)}) %all-reduce.6.cloned.1.call-update) | async-done | bytes 4718608 | tf_op jit(solution)/shard_map/psum | solution.py:125
  141.1 3.8 fusion.169
  147.1 2.1 fusion.14
  149.2 17.8 %fusion.18 = f32[1536,768]{1,0:T(8,128)} fusion(bf16[1536,768]{1,0:T(8,128)(2,1)} %fusion.14, f32[768]{0:T(1024)} %dynamic_slice.23, f32[768,768]{1,0:T(8,128)} %param.31, f32[768,768]{1,0:T(8,128)} %param.30), kind=kOutput, calls=%fused_computation.42 | convolution fusion | flops 3702915072 | bytes 11799552 | tf_op jit(solution)/shard_map/tf,df->td/dot_general | solution.py:131
  170.6 2.0 fusion.35
  172.6 3.1 fusion.177
  175.7 4.6 fusion.175
  183.3 78.0 %all-reduce.8.cloned.1.call-done = f32[1536,768]{1,0:T(8,128)} async-done(((f32[1536,768]{1,0:T(8,128)}), f32[1536,768]{1,0:T(8,128)}) %all-reduce.8.cloned.1.call-update) | async-done | bytes 4718608 | tf_op jit(solution)/shard_map/psum | solution.py:132
  261.3 4.7 fusion.168
  266.1 2.2 copy-done.4
  268.3 2.1 fusion.176
  270.4 2.0 multiply_reduce_fusion.8
  275.7 4.8 fusion.182
  282.6 33.8 %all-reduce.10.cloned.1.call-done = f32[240,768]{1,0:T(8,128)} async-done(((f32[240,768]{1,0:T(8,128)}), f32[240,768]{1,0:T(8,128)}) %all-reduce.10.cloned.1.call-update) | async-done | bytes 737296 | tf_op jit(solution)/shard_map/psum | solution.py:176
  316.4 2.2 fusion.165
  322.6 2.0 fusion.181
  337.6 4.4 fusion.183
  342.0 3.0 copy.97
  345.0 1.9 fusion.91
  347.1 4.6 fusion.64
  353.5 6.1 convolution_bitcast_fusion
  365.9 48.6 %reduce-scatter.5.cloned.1.call-done = f32[96,3,192]{2,0,1:T(8,128)} async-done(((f32[768,3,192]{2,0,1:T(8,128)}), f32[96,3,192]{2,0,1:T(8,128)}) %reduce-scatter.5.cloned.1.call-update) | async-done | bytes 221200 | tf_op jit(solution)/shard_map/reduce_scatter | solution.py:252
  414.5 2.1 fusion.106
  416.7 3.0 multiply_reduce_fusion
  419.8 4.0 add_convert_fusion
  424.4 40.9 %all-reduce = (f32[2,768]{1,0:T(2,128)S(1)}, f32[6,768]{1,0:T(8,128)S(1)}, f32[3072]{0:T(1024)S(1)}) all-reduce(f32[2,768]{1,0:T(2,128)S(1)} %maximum_multiply_fusion, f32[6,768]{1,0:T(8,128)S(1)} %stack.112, f32[3072]{0:T(1024)S(1)} %dynamic_update_slice.13), channel_id=1, replica_groups=mesh['dp'=8,'tensor'=4] {'dp','tensor'}, use_global_device_ids=true, to_apply=%region_27.28 | all-reduce | flops 9216 | bytes 73728 | tf_op jit(solution)/shard_map/psum | solution.py:245
  468.5 18.8 %reduce-scatter.9.cloned.1.call-done = f32[96,768]{1,0:T(8,128)} async-done(((f32[768,768]{1,0:T(8,128)}), f32[96,768]{1,0:T(8,128)}) %reduce-scatter.9.cloned.1.call-update) | async-done | bytes 294928 | tf_op jit(solution)/shard_map/reduce_scatter | solution.py:252
  487.2 2.0 fusion.107
  489.3 4.3 fusion.49
  493.6 65.0 %reduce-scatter.11.cloned.1.call-done = f32[96,768]{1,0:T(8,128)} async-done(((f32[768,768]{1,0:T(8,128)}), f32[96,768]{1,0:T(8,128)}) %reduce-scatter.11.cloned.1.call-update) | async-done | bytes 294928 | tf_op jit(solution)/shard_map/reduce_scatter | solution.py:252
  561.2 6.3 collective-permute-done
  568.4 55.7 %reduce-scatter.7.cloned.1.call-done = f32[96,192]{1,0:T(8,128)} async-done(((f32[768,192]{1,0:T(8,128)}), f32[96,192]{1,0:T(8,128)}) %reduce-scatter.7.cloned.1.call-update) | async-done | bytes 73744 | tf_op jit(solution)/shard_map/reduce_scatter | solution.py:252
  625.2 32.4 %all_gather.10 = f32[768,192]{1,0:T(8,128)S(1)} all-gather(f32[96,192]{1,0:T(8,128)S(1)} %get-tuple-element.109), channel_id=1, replica_groups=mesh['dp'=8,'tensor'=4] {'dp'}, dimensions={0}, use_global_device_ids=true | all-gather | bytes 663552 | tf_op jit(solution)/shard_map/all_gather | solution.py:275
  660.7 59.0 %all-reduce.12.cloned.1.call-done = f32[1536,768]{1,0:T(8,128)} async-done(((f32[1536,768]{1,0:T(8,128)}), f32[1536,768]{1,0:T(8,128)}) %all-reduce.12.cloned.1.call-update) | async-done | bytes 4718608 | tf_op jit(solution)/shard_map/psum | solution.py:224
  719.7 6.6 bitcast_add_fusion
  730.6 43.6 %all-gather.3.cloned.1.call-done = f32[768,3,192]{2,0,1:T(8,128)} async-done(((f32[96,3,192]{2,0,1:T(8,128)}), f32[768,3,192]{2,0,1:T(8,128)}) %all-gather.3.cloned.1.call-update) | async-done | bytes 1769488 | tf_op jit(solution)/shard_map/all_gather | solution.py:274
  774.2 2.9 copy.102
  777.1 50.6 %all-gather.5.cloned.1.call-done = f32[768,768]{1,0:T(8,128)} async-done(((f32[96,768]{1,0:T(8,128)}), f32[768,768]{1,0:T(8,128)}) %all-gather.5.cloned.1.call-update) | async-done | bytes 2359312 | tf_op jit(solution)/shard_map/all_gather | solution.py:276
  827.7 3.2 copy.180
  (243 shorter events, 66.2 us)
Async XLA Ops:
  7.2 263.3 %copy-start = (bf16[1536,768]{1,0:T(8,128)(2,1)S(1)}, bf16[1536,768]{1,0:T(8,128)(2,1)}, u32[]{:S(2)}) copy-start(bf16[1536,768]{1,0:T(8,128)(2,1)} %param.22) | copy-start | bytes 7077892
  7.2 133.9 %all-reduce.6.cloned.1.call-start = ((), (), s32[]{:S(2)}) async-start(), calls=%async_computation.4 | async-start | bytes 9437184 | tf_op jit(solution)/shard_map/psum | solution.py:125
  25.6 7.1 copy-start.53
  34.4 5.7 copy-start.15
  34.5 6.7 copy-start.19
  44.2 217.1 %all-reduce.8.cloned.1.call-start = ((), (), s32[]{:S(2)}) async-start(), calls=%async_computation.5 | async-start | bytes 9437184 | tf_op jit(solution)/shard_map/psum | solution.py:132
  167.0 149.4 %all-reduce.10.cloned.1.call-start = ((), (), s32[]{:S(2)}) async-start(), calls=%async_computation.6 | async-start | bytes 1474560 | tf_op jit(solution)/shard_map/psum | solution.py:176
  172.6 9.3 %copy-start.26 = (bf16[3,80,192]{1,2,0:T(8,128)(2,1)}, bf16[3,80,192]{1,2,0:T(8,128)(2,1)S(1)}, u32[]{:S(2)}) copy-start(bf16[3,80,192]{1,2,0:T(8,128)(2,1)S(1)} %fusion.35) | copy-start | bytes 276484
  175.7 5.7 copy-start.10
  175.7 6.2 copy-start.8
  175.7 6.2 copy-start.48
  180.3 81.0 %copy-start.33 = (f32[1536]{0:T(1024)S(1)}, f32[1536]{0:T(1024)}, u32[]{:S(2)}) copy-start(f32[1536]{0:T(1024)} %copy-done.32) | copy-start | bytes 18436
  180.3 81.0 %copy-start.37 = (f32[1536]{0:T(1024)S(1)}, f32[1536]{0:T(1024)}, u32[]{:S(2)}) copy-start(f32[1536]{0:T(1024)} %copy-done.36) | copy-start | bytes 18436
  180.3 81.0 %copy-start.40 = (f32[768]{0:T(1024)S(1)}, f32[768]{0:T(1024)}, u32[]{:S(2)}) copy-start(f32[768]{0:T(1024)} %get-tuple-element.120) | copy-start | bytes 9220
  180.3 81.0 %copy-start.50 = (f32[768]{0:T(1024)S(1)}, f32[768]{0:T(1024)}, u32[]{:S(2)}) copy-start(f32[768]{0:T(1024)} %get-tuple-element.121) | copy-start | bytes 9220
  275.7 4.8 copy-start.17
  275.7 4.8 copy-start.9
  281.9 132.6 %reduce-scatter.5.cloned.1.call-start = ((), (), s32[]{:S(2)}) async-start(), calls=%async_computation.8 | async-start | bytes 2654208 | tf_op jit(solution)/shard_map/reduce_scatter | solution.py:252
  320.3 4.3 copy-start.11
  329.1 8.4 %copy-start.20 = (bf16[1536,1,192]{0,2,1:T(8,128)(2,1)}, bf16[1536,1,192]{0,2,1:T(8,128)(2,1)S(1)}, u32[]{:S(2)}) copy-start(bf16[1536,1,192]{0,2,1:T(8,128)(2,1)S(1)} %stack_reshape.17) | copy-start | bytes 1769476
  345.0 142.3 %reduce-scatter.9.cloned.1.call-start = ((), (), s32[]{:S(2)}) async-start(), calls=%async_computation.11 | async-start | bytes 2654208 | tf_op jit(solution)/shard_map/reduce_scatter | solution.py:252
  347.0 4.7 copy-start.14
  347.0 211.5 %reduce-scatter.11.cloned.1.call-start = ((), (), s32[]{:S(2)}) async-start(), calls=%async_computation.13 | async-start | bytes 2654208 | tf_op jit(solution)/shard_map/reduce_scatter | solution.py:252
  351.7 272.4 %reduce-scatter.7.cloned.1.call-start = ((), (), s32[]{:S(2)}) async-start(), calls=%async_computation.10 | async-start | bytes 884736 | tf_op jit(solution)/shard_map/reduce_scatter | solution.py:252
  353.3 366.4 %all-reduce.12.cloned.1.call-start = ((), (), s32[]{:S(2)}) async-start(), calls=%async_computation.7 | async-start | bytes 9437184 | tf_op jit(solution)/shard_map/psum | solution.py:224
  359.6 5.5 copy-start.38
  359.6 5.5 copy-start.41
  359.6 5.5 copy-start.7
  359.6 5.9 copy-start.49
  359.6 6.0 copy-start.52
  359.6 414.6 %all-gather.3.cloned.1.call-start = ((), (), s32[]{:S(2)}) async-start(), calls=%async_computation.9 | async-start | bytes 2654208 | tf_op jit(solution)/shard_map/all_gather | solution.py:274
  363.1 56.6 %copy-start.44 = (f32[768]{0:T(1024)S(1)}, f32[768]{0:T(1024)}, u32[]{:S(2)}) copy-start(f32[768]{0:T(1024)} %get-tuple-element.122) | copy-start | bytes 9220
  416.6 411.0 %all-gather.5.cloned.1.call-start = ((), (), s32[]{:S(2)}) async-start(), calls=%async_computation.12 | async-start | bytes 2654208 | tf_op jit(solution)/shard_map/all_gather | solution.py:276
  419.7 4.3 copy-start.47
  419.7 4.3 copy-start.46
  419.7 45.6 %copy-start.35 = (f32[6,768]{1,0:T(8,128)S(1)}, f32[6,768]{1,0:T(8,128)}, u32[]{:S(2)}) copy-start(f32[6,768]{1,0:T(8,128)} %param.33) | copy-start | bytes 55300
  419.7 46.9 %copy-start.42 = (f32[2,768]{1,0:T(2,128)S(1)}, f32[2,768]{1,0:T(2,128)}, u32[]{:S(2)}) copy-start(f32[2,768]{1,0:T(2,128)} %param.32) | copy-start | bytes 18436
  419.7 46.9 %copy-start.51 = (f32[2,2,768]{2,1,0:T(2,128)S(1)}, f32[2,2,768]{2,1,0:T(2,128)}, u32[]{:S(2)}) copy-start(f32[2,2,768]{2,1,0:T(2,128)} %param.39) | copy-start | bytes 36868
  419.7 48.1 %copy-start.43 = (f32[3072]{0:T(1024)S(1)}, f32[3072]{0:T(1024)}, u32[]{:S(2)}) copy-start(f32[3072]{0:T(1024)} %param.34) | copy-start | bytes 36868
  419.8 67.5 %copy-start.28 = (f32[2,96,768]{2,1,0:T(8,128)S(1)}, f32[2,96,768]{2,1,0:T(8,128)}, u32[]{:S(2)}) copy-start(f32[2,96,768]{2,1,0:T(8,128)} %param.37) | copy-start | bytes 1769476
  423.8 134.8 %copy-start.29 = (f32[2,96,768]{2,1,0:T(8,128)S(1)}, f32[2,96,768]{2,1,0:T(8,128)}, u32[]{:S(2)}) copy-start(f32[2,96,768]{2,1,0:T(8,128)} %param.38) | copy-start | bytes 1769476
  489.3 134.9 %copy-start.30 = (f32[96,192]{1,0:T(8,128)S(1)}, f32[96,192]{1,0:T(8,128)}, u32[]{:S(2)}) copy-start(f32[96,192]{1,0:T(8,128)} %copy.109) | copy-start | bytes 221188
  559.8 7.7 collective-permute-start
  567.7 91.7 %collective-permute-start.1 = (f32[2,96,768]{2,1,0:T(8,128)S(1)}, f32[2,96,768]{2,1,0:T(8,128)}, u32[]{:S(2)}, u32[]{:S(2)}) collective-permute-start(f32[2,96,768]{2,1,0:T(8,128)S(1)} %get-tuple-element.106), channel_id=1, source_target_pairs={{0,8},{4,12},{8,0},{12,4},{16,24},{20,28},{24,16},{28,20},{1,9},{5... | collective-permute-start | bytes 1769480 | tf_op jit(solution)/shard_map/ppermute | solution.py:27
  660.6 68.2 %collective-permute-start.2 = (f32[4,96,768]{2,1,0:T(8,128)S(1)}, f32[4,96,768]{2,1,0:T(8,128)S(1)}, u32[]{:S(2)}, u32[]{:S(2)}) collective-permute-start(f32[4,96,768]{2,1,0:T(8,128)S(1)} %bitcast.220), channel_id=1, source_target_pairs={{0,16},{4,20},{8,24},{12,28},{16,0},{20,4},{24,8},{28,12},{1,17},{... | collective-permute-start | bytes 3538952 | tf_op jit(solution)/shard_map/ppermute | solution.py:27
  719.6 6.6 copy-start.24
  719.6 6.6 copy-start.25
  729.0 101.9 %copy-start.1 = (bf16[1536,768]{1,0:T(8,128)(2,1)S(1)}, bf16[1536,768]{1,0:T(8,128)(2,1)}, u32[]{:S(2)}) copy-start(bf16[1536,768]{1,0:T(8,128)(2,1)} %param.22) | copy-start | bytes 7077892
  (20 other events, 42.6 us)
Sparse Core Ops, SparseCore 0:
  44.4 96.7 all-reduce.5
  167.1 94.1 all-reduce.7
  282.0 34.3 all-reduce.9
  345.1 69.3 reduce-scatter.4
  418.4 68.8 reduce-scatter.8
  490.6 67.8 reduce-scatter.10
  562.4 61.6 reduce-scatter.6
  626.6 92.9 all-reduce.11
  722.1 52.0 all-gather.2
  777.0 50.5 all-gather.4
